TPU v7x, 32 devices: a whole 2x2x4 slice. The times are simulated.
32 devices in a mesh: seq: 16 (over z, x, core), fsdp: 2 (over y).
Axes of the slice: x: 2, y: 2, z: 4, core: 2. Of those that a mesh axis runs over, the one named last changes fastest.
Arguments:
- inputs: bfloat16 [2, 128, 16, 4096], P('fsdp', None, 'seq'), may hold values from -6 to 6
- queries: bfloat16 [2, 128, 16, 4096], P('fsdp', None, 'seq'), may hold values from -1000 to 1000
- rotated_keys: bfloat16 [2, 128, 16, 512], P('fsdp', None, 'seq'), may hold values from -6 to 6
- out_grad: bfloat16 [2, 128, 16, 4096], P('fsdp', None, 'seq'), may hold values from -6 to 6
- value_weight: bfloat16 [4096, 512], P(('seq', 'fsdp')), may hold values from -0.09375 to 0.09375
- fisher: float32 [4096, 512], P(('seq', 'fsdp')), may hold values from 0.2 to 20
- anchor: float32 [4096, 512], P(('seq', 'fsdp')), may hold values from -0.25 to 0.25
- doc_starts: int32 [2, 32], P('fsdp'), may hold values from 0 to 2032, as said below
- owners: int32 [2, 32], P('fsdp'), may hold values from 0 to 15, as said below
Outputs:
- query_grad: bfloat16 [2, 16, 12, 16, 4096], P('fsdp', 'seq')
- key_grad: bfloat16 [2, 128, 16, 512], P('fsdp', None, 'seq')
- input_grad: bfloat16 [2, 128, 16, 4096], P('fsdp', None, 'seq')
- ewc_grad: float32 [4096, 512], P(('seq', 'fsdp'))
Inputs may be any that keep to these rules, and one draw needn't show every extreme that they name: `doc_starts`: in each sequence the starts rise strictly from 0; every document's length (2048 minus the last start for the last one) is a multiple of 16. Each of the 16 owners is named by exactly two documents of a sequence; one owner's documents hold at most 192 positions in all, and in every sequence some owner holds exactly that many.
All inputs are finite; a program needn't handle non-finite values.
Results may differ from a plain program's by a relative error of at most 0.029.
Values may be sent and summed in bfloat16 or wider, within the bound.
A program may use at most 128 MiB of HBM per device.

v0:
```python
import math

import jax
import jax.numpy as jnp
from jax import lax
from jax.sharding import PartitionSpec as P

KVH = 4
HD = 128


SCORE_NEG = -1e30
EWC_LAMBDA = 4.0


def round_plan(starts, owner_list, lane_count, rounds):
    round_ids = jnp.arange(rounds, dtype=jnp.int32)
    start_rounds = starts // lane_count
    doc_of = jnp.sum((start_rounds[None, :] <= round_ids[:, None]).astype(jnp.int32), axis=1) - 1
    doc_ids = jnp.arange(starts.shape[0], dtype=jnp.int32)
    onehot = (doc_of[:, None] == doc_ids[None, :]).astype(jnp.int32)
    owner_of = jnp.sum(onehot * owner_list[None, :], axis=1)
    earlier = (owner_of[:, None] == owner_of[None, :]) & (round_ids[None, :] < round_ids[:, None])
    rank_of = jnp.sum(earlier.astype(jnp.int32), axis=1)
    return (doc_of, owner_of, rank_of)


def slot_rounds(owner_of, rank_of, lane_count, capacity):
    lane_ids = jnp.arange(lane_count, dtype=jnp.int32)
    slot_ids = jnp.arange(capacity, dtype=jnp.int32)
    round_ids = jnp.arange(owner_of.shape[0], dtype=jnp.int32)
    match = (owner_of[None, None, :] == lane_ids[None, :, None]) & (
        rank_of[None, None, :] == slot_ids[:, None, None]
    )
    source = jnp.sum(match.astype(jnp.int32) * round_ids[None, None, :], axis=2)
    filled = jnp.any(match, axis=2)
    return (source, filled)


def attend(query_in, grad_in, key_in, value_in, visible):
    slot_count = query_in.shape[0] * query_in.shape[1]
    group = query_in.shape[3] // HD
    scale = 1.0 / math.sqrt(HD)
    query_parts = []
    key_parts = []
    value_parts = []
    for item_index in range(query_in.shape[2]):
        q_item = query_in[:, :, item_index, :].reshape(slot_count, group, HD)
        g_item = grad_in[:, :, item_index, :].reshape(slot_count, group, HD)
        k_item = key_in[:, :, item_index, :].reshape(slot_count, HD)
        v_item = value_in[:, :, item_index, :].reshape(slot_count, HD)
        scores = (
            jnp.einsum("mgd,kd->gmk", q_item, k_item, preferred_element_type=jnp.float32) * scale
        )
        masked = jnp.where(visible[None], scores, SCORE_NEG)
        peak = jnp.max(masked, axis=2, keepdims=True)
        probs = jnp.where(visible[None], jnp.exp(masked - peak), 0.0)
        totals = jnp.sum(probs, axis=2, keepdims=True)
        probs = probs / jnp.where(totals > 0.0, totals, 1.0)
        probs_b = probs.astype(jnp.bfloat16)
        attn_out = jnp.einsum(
            "gmk,kd->mgd", probs_b, v_item, preferred_element_type=jnp.float32
        ).astype(jnp.bfloat16)
        delta = jnp.einsum("mgd,mgd->gm", g_item, attn_out, preferred_element_type=jnp.float32)
        dprobs = jnp.einsum("mgd,kd->gmk", g_item, v_item, preferred_element_type=jnp.float32)
        dscores = (probs * (dprobs - delta[:, :, None]) * scale).astype(jnp.bfloat16)
        query_grad = jnp.einsum(
            "gmk,kd->mgd", dscores, k_item, preferred_element_type=jnp.float32
        ).astype(jnp.bfloat16)
        key_grad = jnp.einsum(
            "gmk,mgd->kd", dscores, q_item, preferred_element_type=jnp.float32
        ).astype(jnp.bfloat16)
        value_grad = jnp.einsum(
            "gmk,mgd->kd", probs_b, g_item, preferred_element_type=jnp.float32
        ).astype(jnp.bfloat16)
        query_parts.append(query_grad.reshape(query_in.shape[0], query_in.shape[1], group * HD))
        key_parts.append(key_grad.reshape(query_in.shape[0], query_in.shape[1], HD))
        value_parts.append(value_grad.reshape(query_in.shape[0], query_in.shape[1], HD))
    return (
        jnp.stack(query_parts, axis=2),
        jnp.stack(key_parts, axis=2),
        jnp.stack(value_parts, axis=2),
    )


def fetch_weight(value_weight):
    return lax.all_gather(value_weight, ("seq", "fsdp"), axis=0, tiled=True)


def body(inputs, queries, rotated_keys, out_grad, value_weight, fisher, anchor, doc_starts, owners):
    lane_count = lax.axis_size("seq")
    own_lane = lax.axis_index("seq")
    rounds = inputs.shape[1]
    capacity = 3 * rounds // (2 * lane_count)
    token_rows = inputs.reshape(rounds, inputs.shape[3])
    query_rows = queries.reshape(rounds, queries.shape[3])
    key_rows = rotated_keys.reshape(rounds, rotated_keys.shape[3])
    grad_rows = out_grad.reshape(rounds, out_grad.shape[3])
    doc_of, owner_of, rank_of = round_plan(doc_starts[0], owners[0], lane_count, rounds)
    source, filled = slot_rounds(owner_of, rank_of, lane_count, capacity)

    def to_slots(rows):
        picked = jnp.take(rows, source.reshape(-1), axis=0).reshape(capacity, lane_count, KVH, -1)
        return jnp.where(filled[:, :, None, None], picked, jnp.zeros_like(picked))

    query_send = to_slots(query_rows)
    grad_send = to_slots(grad_rows)
    key_send = to_slots(key_rows)
    my_rounds = lax.dynamic_index_in_dim(source, own_lane, 1, keepdims=False)
    my_filled = lax.dynamic_index_in_dim(filled, own_lane, 1, keepdims=False)
    lane_ids = jnp.arange(lane_count, dtype=jnp.int32)
    slot_pos = (my_rounds[:, None] * lane_count + lane_ids[None, :]).reshape(-1)
    round_doc = jnp.where(my_filled, jnp.take(doc_of, my_rounds), -1)
    slot_doc = jnp.broadcast_to(round_doc[:, None], (capacity, lane_count)).reshape(-1)
    slot_live = jnp.broadcast_to(my_filled[:, None], (capacity, lane_count)).reshape(-1)
    visible = (slot_doc[:, None] == slot_doc[None, :]) & (slot_pos[None, :] <= slot_pos[:, None])
    visible = visible & slot_live[:, None] & slot_live[None, :]
    full_weight = fetch_weight(value_weight)
    value_rows = jnp.dot(token_rows, full_weight, preferred_element_type=jnp.float32).astype(
        jnp.bfloat16
    )
    value_send = to_slots(value_rows)
    query_back, key_back, value_back = attend(
        lax.all_to_all(query_send, "seq", split_axis=1, concat_axis=1, tiled=True),
        lax.all_to_all(grad_send, "seq", split_axis=1, concat_axis=1, tiled=True),
        lax.all_to_all(key_send, "seq", split_axis=1, concat_axis=1, tiled=True),
        lax.all_to_all(value_send, "seq", split_axis=1, concat_axis=1, tiled=True),
        visible,
    )
    returned = (
        lax.all_to_all(key_back, "seq", split_axis=1, concat_axis=1, tiled=True),
        lax.all_to_all(value_back, "seq", split_axis=1, concat_axis=1, tiled=True),
    )
    flat_index = rank_of * lane_count + owner_of
    key_home = jnp.take(returned[0].reshape(capacity * lane_count, -1), flat_index, axis=0)
    value_home = jnp.take(returned[1].reshape(capacity * lane_count, -1), flat_index, axis=0)
    input_grad = jnp.einsum(
        "rk,dk->rd", value_home, full_weight, preferred_element_type=jnp.float32
    ).astype(jnp.bfloat16)
    partial_sum = jnp.einsum(
        "rd,rk->dk", token_rows, value_home, preferred_element_type=jnp.float32
    )
    summed = lax.psum_scatter(partial_sum, ("seq", "fsdp"), scatter_dimension=0, tiled=True)
    tokens_total = rounds * lane_count * lax.axis_size("fsdp")
    grad_scale = 1.0 / math.sqrt(tokens_total)
    ewc_grad = summed * grad_scale + EWC_LAMBDA * fisher * (
        value_weight.astype(jnp.float32) - anchor
    )
    query_out = query_back.reshape(1, 1, capacity, lane_count, -1)
    return (
        query_out,
        key_home.reshape(1, rounds, 1, -1),
        input_grad.reshape(1, rounds, 1, -1),
        ewc_grad,
    )


def solution(mesh):
    return jax.shard_map(
        body,
        mesh=mesh,
        in_specs=(
            P("fsdp", None, "seq", None),
            P("fsdp", None, "seq", None),
            P("fsdp", None, "seq", None),
            P("fsdp", None, "seq", None),
            P(("seq", "fsdp"), None),
            P(("seq", "fsdp"), None),
            P(("seq", "fsdp"), None),
            P("fsdp", None),
            P("fsdp", None),
        ),
        out_specs=(
            P("fsdp", "seq", None, None, None),
            P("fsdp", None, "seq", None),
            P("fsdp", None, "seq", None),
            P(("seq", "fsdp"), None),
        ),
        check_vma=False,
    )
```

profile of v0, /device:TPU:0, one launch (start us, length us, event | category | flops | bytes accessed | tf_op | source)
XLA Modules:
  0.0 374.4 jit_solution(6865319597100991521)
XLA Ops:
  10.9 5.6 %gather_fusion.4 = bf16[192,4096]{1,0:T(8,128)(2,1)} fusion(bf16[128,4096]{1,0:T(8,128)(2,1)} %bitcast.290, s32[1024]{0:T(1024)S(1)} %pad_clamp_fusion.2), kind=kCustom, calls=%fused_computation.4.clone | custom fusion | bytes 3146496 | tf_op jit(solution)/shard_map/jit(_take)/gather | solution.py:103
  16.6 2.7 gather_fusion.2
  19.3 3.9 %broadcast_select_fusion = (bf16[192,4096]{1,0:T(8,128)(2,1)}, bf16[192,4096]{1,0:T(8,128)(2,1)}) fusion(bf16[192,4096]{1,0:T(8,128)(2,1)} %gather_fusion.4, pred[192]{0:T(512)(128)(4,1)S(1)} %compare_and_fusion.1, bf16[192,4096]{1,0:T(8,128)(2,1)} %gather_fusion.2), kind=kLoop, calls=%fused_computation.45 | loop fusion | flops 1572864 | bytes 6291648 | tf_op jit(solution)/shard_map/jit(_take)/select_n | solution.py:103
  23.2 2.9 reshape.287
  26.1 3.9 %reshape.283 = bf16[12,16,4,1024]{3,2,1,0:T(4,128)(2,1)} reshape(bf16[192,4096]{1,0:T(8,128)(2,1)} %get-tuple-element.60) | data formatting | bytes 3145728 | tf_op jit(solution)/shard_map/reshape | solution.py:103
  30.0 3.6 copy_select_fusion
  33.6 58.6 %all_to_all.30 = bf16[12,16,4,1024]{3,2,0,1:T(4,128)(2,1)} all-to-all(bf16[12,16,4,1024]{3,2,0,1:T(4,128)(2,1)S(1)} %get-tuple-element.56), channel_id=1, replica_groups=mesh['seq'=16,'fsdp'=2] {'seq'}, dimensions={1} | all-to-all | bytes 3145728 | tf_op jit(solution)/shard_map/all_to_all | solution.py:124
  92.3 5.4 %all-to-all-start.3 = ((bf16[12,16,4,1024]{3,2,0,1:T(4,128)(2,1)}), bf16[12,16,4,1024]{3,2,0,1:T(4,128)(2,1)S(1)}, u32[]{:S(2)}, u32[]{:S(2)}) async-start(bf16[12,16,4,1024]{3,2,0,1:T(4,128)(2,1)} %get-tuple-element.55), calls=%async_computation.3 | async-start | bytes 3145728 | tf_op jit(solution)/shard_map/all_to_all | solution.py:125
  101.3 6.6 %fusion.106 = (bf16[12,16,1,1024]{3,2,0,1:T(2,128)(2,1)S(1)}, bf16[12,16,1,1024]{3,2,0,1:T(2,128)(2,1)S(1)}, bf16[12,16,1,1024]{3,2,0,1:T(2,128)(2,1)S(1)}, bf16[12,16,1,1024]{3,2,0,1:T(2,128)(2,1)S(1)}) fusion(bf16[12,16,4,1024]{3,2,0,1:T(4,128)(2,1)} %all_to_all.30), kind=kLoop, calls=%fused_computation.184 | loop fusion | bytes 3145728 | tf_op jit(solution)/shard_map/slice | solution.py:48
  112.9 2.9 convolution_convert_fusion.9
  118.1 11.6 %all-to-all-done.3 = bf16[12,16,4,1024]{3,2,0,1:T(4,128)(2,1)S(1)} async-done(((bf16[12,16,4,1024]{3,2,0,1:T(4,128)(2,1)}), bf16[12,16,4,1024]{3,2,0,1:T(4,128)(2,1)S(1)}, u32[]{:S(2)}, u32[]{:S(2)}) %all-to-all-start.3) | async-done | bytes 1572896 | tf_op jit(solution)/shard_map/all_to_all | solution.py:125
  129.6 9.3 %all-to-all-start = ((bf16[12,16,4,128]{3,2,0,1:T(4,128)(2,1)}), bf16[12,16,4,128]{3,2,0,1:T(4,128)(2,1)S(1)}, u32[]{:S(2)}, u32[]{:S(2)}) async-start(bf16[12,16,4,128]{3,2,0,1:T(4,128)(2,1)} %get-tuple-element.58), calls=%async_computation | async-start | bytes 393216 | tf_op jit(solution)/shard_map/all_to_all | solution.py:126
  138.9 3.3 fusion.105
  164.6 4.8 %all-to-all-start.5 = ((bf16[12,16,4,128]{3,2,0,1:T(4,128)(2,1)}), bf16[12,16,4,128]{3,2,0,1:T(4,128)(2,1)S(1)}, u32[]{:S(2)}, u32[]{:S(2)}) async-start(bf16[12,16,4,128]{3,2,0,1:T(4,128)(2,1)} %pad_maximum_fusion.2), calls=%async_computation.5 | async-start | bytes 393216 | tf_op jit(solution)/shard_map/all_to_all | solution.py:132
  169.5 8.9 %all-to-all-done.5 = bf16[12,16,4,128]{3,2,0,1:T(4,128)(2,1)S(1)} async-done(((bf16[12,16,4,128]{3,2,0,1:T(4,128)(2,1)}), bf16[12,16,4,128]{3,2,0,1:T(4,128)(2,1)S(1)}, u32[]{:S(2)}, u32[]{:S(2)}) %all-to-all-start.5) | async-done | bytes 196640 | tf_op jit(solution)/shard_map/all_to_all | solution.py:132
  179.4 4.6 %convolution_bitcast_fusion = f32[4096,512]{0,1:T(8,128)} fusion(bf16[1,128,1,4096]{3,1,2,0:T(8,128)(2,1)S(1)} %copy-done, bf16[128,512]{1,0:T(8,128)(2,1)S(1)} %gather_fusion.6, pred[128]{0:T(512)(128)(4,1)S(1)} %get-tuple-element.37), kind=kOutput, calls=%fused_computation.11 | convolution fusion | flops 536936448 | bytes 9568384 | tf_op jit(solution)/shard_map/rd,rk->dk/dot_general | solution.py:140
  187.5 3.7 %all-to-all-start.2 = ((bf16[12,16,4,128]{3,2,0,1:T(4,128)(2,1)}), bf16[12,16,4,128]{3,2,0,1:T(4,128)(2,1)S(1)}, u32[]{:S(2)}, u32[]{:S(2)}) async-start(bf16[12,16,4,128]{3,2,0,1:T(4,128)(2,1)} %get-tuple-element.57), calls=%async_computation.2 | async-start | bytes 393216 | tf_op jit(solution)/shard_map/all_to_all | solution.py:127
  192.5 7.8 %all-to-all-done.2 = bf16[12,16,4,128]{3,2,0,1:T(4,128)(2,1)S(1)} async-done(((bf16[12,16,4,128]{3,2,0,1:T(4,128)(2,1)}), bf16[12,16,4,128]{3,2,0,1:T(4,128)(2,1)S(1)}, u32[]{:S(2)}, u32[]{:S(2)}) %all-to-all-start.2) | async-done | bytes 196640 | tf_op jit(solution)/shard_map/all_to_all | solution.py:127
  205.0 1.9 stack_reshape.37
  222.3 4.1 %all-to-all-start.4 = ((bf16[12,16,4,128]{3,2,0,1:T(4,128)(2,1)}), bf16[12,16,4,128]{3,2,0,1:T(4,128)(2,1)S(1)}, u32[]{:S(2)}, u32[]{:S(2)}) async-start(bf16[12,16,4,128]{3,2,0,1:T(4,128)(2,1)} %pad_maximum_fusion.1), calls=%async_computation.4 | async-start | bytes 393216 | tf_op jit(solution)/shard_map/all_to_all | solution.py:131
  228.8 2.4 reshape.288
  231.1 4.2 %all-to-all-done.4 = bf16[12,16,4,128]{3,2,0,1:T(4,128)(2,1)S(1)} async-done(((bf16[12,16,4,128]{3,2,0,1:T(4,128)(2,1)}), bf16[12,16,4,128]{3,2,0,1:T(4,128)(2,1)S(1)}, u32[]{:S(2)}, u32[]{:S(2)}) %all-to-all-start.4) | async-done | bytes 196640 | tf_op jit(solution)/shard_map/all_to_all | solution.py:131
  237.2 4.8 %fusion.4 = bf16[1,128,1,4096]{3,1,2,0:T(8,128)(2,1)} fusion(bf16[4096,512]{1,0:T(8,128)(2,1)} %all-gather.2.cloned.1.call-done, bf16[128,512]{1,0:T(8,128)(2,1)S(1)} %gather_fusion.6, pred[128]{0:T(512)(128)(4,1)S(1)} %copy-done.59), kind=kOutput, calls=%fused_computation.13 | convolution fusion | flops 537460736 | bytes 5374080 | tf_op jit(solution)/shard_map/rk,dk->rd/dot_general | solution.py:137
  242.0 123.4 %reduce-scatter.2.cloned.1.call-done = f32[128,512]{0,1:T(8,128)} async-done(((f32[4096,512]{0,1:T(8,128)}), f32[128,512]{0,1:T(8,128)}) %reduce-scatter.2.cloned.1.call-update) | async-done | bytes 262160 | tf_op jit(solution)/shard_map/reduce_scatter | solution.py:143
  (264 shorter events, 67.9 us)
Async XLA Ops:
  7.2 105.7 %copy-start = (bf16[1,128,1,4096]{3,1,2,0:T(8,128)(2,1)S(1)}, bf16[1,128,1,4096]{3,1,2,0:T(8,128)(2,1)}, u32[]{:S(2)}) copy-start(bf16[1,128,1,4096]{3,1,2,0:T(8,128)(2,1)} %param.15) | copy-start | bytes 3145732
  7.2 105.7 %all-gather.2.cloned.1.call-start = ((), (), s32[]{:S(2)}) async-start(), calls=%async_computation.7 | async-start | bytes 4325376 | tf_op jit(solution)/shard_map/all_gather | solution.py:87
  10.9 5.7 %copy-start.2 = (bf16[1,128,1,4096]{3,1,2,0:T(8,128)(2,1)S(1)}, bf16[1,128,1,4096]{3,1,2,0:T(8,128)(2,1)}, u32[]{:S(2)}) copy-start(bf16[1,128,1,4096]{3,1,2,0:T(8,128)(2,1)} %param.16) | copy-start | bytes 3145732
  92.3 7.2 %copy-start.3 = (bf16[1,128,1,512]{3,1,2,0:T(8,128)(2,1)S(1)}, bf16[1,128,1,512]{3,1,2,0:T(8,128)(2,1)}, u32[]{:S(2)}) copy-start(bf16[1,128,1,512]{3,1,2,0:T(8,128)(2,1)} %param.17) | copy-start | bytes 393220
  92.3 37.4 %all-to-all-start.3 = ((bf16[12,16,4,1024]{3,2,0,1:T(4,128)(2,1)}), bf16[12,16,4,1024]{3,2,0,1:T(4,128)(2,1)S(1)}, u32[]{:S(2)}, u32[]{:S(2)}) async-start(bf16[12,16,4,1024]{3,2,0,1:T(4,128)(2,1)} %get-tuple-element.55), calls=%async_computation.3 | async-start | bytes 3145728 | tf_op jit(solution)/shard_map/all_to_all | solution.py:125
  129.6 18.3 %all-to-all-start = ((bf16[12,16,4,128]{3,2,0,1:T(4,128)(2,1)}), bf16[12,16,4,128]{3,2,0,1:T(4,128)(2,1)S(1)}, u32[]{:S(2)}, u32[]{:S(2)}) async-start(bf16[12,16,4,128]{3,2,0,1:T(4,128)(2,1)} %get-tuple-element.58), calls=%async_computation | async-start | bytes 393216 | tf_op jit(solution)/shard_map/all_to_all | solution.py:126
  142.8 19.2 %copy-start.21 = (bf16[24,8,8,128]{3,2,1,0:T(8,128)(2,1)}, bf16[24,8,8,128]{3,2,1,0:T(8,128)(2,1)S(1)}, u32[]{:S(2)}) copy-start(bf16[24,8,8,128]{3,2,1,0:T(8,128)(2,1)S(1)} %copy.399) | copy-start | bytes 1179652
  148.2 11.8 %copy-start.43 = (bf16[12,16,1,128]{3,1,0,2:T(8,128)(2,1)}, bf16[12,16,1,128]{3,1,0,2:T(8,128)(2,1)S(1)}, u32[]{:S(2)}) copy-start(bf16[12,16,1,128]{3,1,0,2:T(8,128)(2,1)S(1)} %copy.302) | copy-start | bytes 147460
  148.2 8.1 %copy-start.45 = (bf16[12,16,1,128]{3,1,0,2:T(8,128)(2,1)}, bf16[12,16,1,128]{3,1,0,2:T(8,128)(2,1)S(1)}, u32[]{:S(2)}) copy-start(bf16[12,16,1,128]{3,1,0,2:T(8,128)(2,1)S(1)} %copy.334) | copy-start | bytes 147460
  161.9 7.5 %copy-start.62 = (s32[128]{0:T(128)S(1)}, s32[128]{0:T(128)}, u32[]{:S(2)}) copy-start(s32[128]{0:T(128)} %copy-done.61) | copy-start | bytes 1540
  162.0 7.5 %copy-start.64 = (s32[128]{0:T(128)S(1)}, s32[128]{0:T(128)}, u32[]{:S(2)}) copy-start(s32[128]{0:T(128)} %copy-done.63) | copy-start | bytes 1540
  164.6 13.8 %all-to-all-start.5 = ((bf16[12,16,4,128]{3,2,0,1:T(4,128)(2,1)}), bf16[12,16,4,128]{3,2,0,1:T(4,128)(2,1)S(1)}, u32[]{:S(2)}, u32[]{:S(2)}) async-start(bf16[12,16,4,128]{3,2,0,1:T(4,128)(2,1)} %pad_maximum_fusion.2), calls=%async_computation.5 | async-start | bytes 393216 | tf_op jit(solution)/shard_map/all_to_all | solution.py:132
  169.4 196.0 %reduce-scatter.2.cloned.1.call-start = ((), (), s32[]{:S(2)}) async-start(), calls=%async_computation.8 | async-start | bytes 8650752 | tf_op jit(solution)/shard_map/reduce_scatter | solution.py:143
  169.5 14.5 %copy-start.58 = (pred[128]{0:T(512)(128)(4,1)}, pred[128]{0:T(512)(128)(4,1)S(1)}, u32[]{:S(2)}) copy-start(pred[128]{0:T(512)(128)(4,1)S(1)} %get-tuple-element.37) | copy-start | bytes 388
  169.5 14.5 %copy-start.60 = (s32[1024]{0:T(1024)}, s32[1024]{0:T(1024)S(1)}, u32[]{:S(2)}) copy-start(s32[1024]{0:T(1024)S(1)} %pad_clamp_fusion) | copy-start | bytes 12292
  187.5 12.7 %all-to-all-start.2 = ((bf16[12,16,4,128]{3,2,0,1:T(4,128)(2,1)}), bf16[12,16,4,128]{3,2,0,1:T(4,128)(2,1)S(1)}, u32[]{:S(2)}, u32[]{:S(2)}) async-start(bf16[12,16,4,128]{3,2,0,1:T(4,128)(2,1)} %get-tuple-element.57), calls=%async_computation.2 | async-start | bytes 393216 | tf_op jit(solution)/shard_map/all_to_all | solution.py:127
  192.4 9.7 %copy-start.57 = (f32[8,192]{1,0:T(8,128)S(1)}, f32[8,192]{1,0:T(8,128)}, u32[]{:S(2)}) copy-start(f32[8,192]{1,0:T(8,128)} %copy-done.56) | copy-start | bytes 18436
  201.2 12.6 %copy-start.52 = (bf16[12,16,1,128]{3,1,0,2:T(8,128)(2,1)}, bf16[12,16,1,128]{3,1,0,2:T(8,128)(2,1)S(1)}, u32[]{:S(2)}) copy-start(bf16[12,16,1,128]{3,1,0,2:T(8,128)(2,1)S(1)} %copy.337) | copy-start | bytes 147460
  220.7 5.7 %copy-start.44 = (bf16[12,16,1,128]{3,1,0,2:T(8,128)(2,1)S(1)}, bf16[12,16,1,128]{3,1,0,2:T(8,128)(2,1)}, u32[]{:S(2)}) copy-start(bf16[12,16,1,128]{3,1,0,2:T(8,128)(2,1)} %copy-done.43) | copy-start | bytes 147460
  222.3 13.0 %all-to-all-start.4 = ((bf16[12,16,4,128]{3,2,0,1:T(4,128)(2,1)}), bf16[12,16,4,128]{3,2,0,1:T(4,128)(2,1)S(1)}, u32[]{:S(2)}, u32[]{:S(2)}) async-start(bf16[12,16,4,128]{3,2,0,1:T(4,128)(2,1)} %pad_maximum_fusion.1), calls=%async_computation.4 | async-start | bytes 393216 | tf_op jit(solution)/shard_map/all_to_all | solution.py:131
  237.2 128.2 %copy-start.32 = (f32[128,512]{0,1:T(8,128)S(1)}, f32[128,512]{0,1:T(8,128)}, u32[]{:S(2)}) copy-start(f32[128,512]{0,1:T(8,128)} %copy.362) | copy-start | bytes 786436
  237.2 128.3 %copy-start.33 = (f32[128,512]{0,1:T(8,128)S(1)}, f32[128,512]{0,1:T(8,128)}, u32[]{:S(2)}) copy-start(f32[128,512]{0,1:T(8,128)} %copy.364) | copy-start | bytes 786436
  237.2 128.3 %copy-start.37 = (bf16[128,512]{0,1:T(8,128)(2,1)S(1)}, bf16[128,512]{0,1:T(8,128)(2,1)}, u32[]{:S(2)}) copy-start(bf16[128,512]{0,1:T(8,128)(2,1)} %copy.363) | copy-start | bytes 393220
  237.2 130.1 %copy-start.1 = (bf16[1,128,1,4096]{3,1,2,0:T(8,128)(2,1)S(1)}, bf16[1,128,1,4096]{3,1,2,0:T(8,128)(2,1)}, u32[]{:S(2)}) copy-start(bf16[1,128,1,4096]{3,1,2,0:T(8,128)(2,1)} %param.15) | copy-start | bytes 3145732
  (48 other events, 98.0 us)
Sparse Core Ops, SparseCore 0:
  10.9 78.7 all-gather.1
  184.2 181.2 reduce-scatter.1
where the time goes:
time: 381 us; the launch traced here: 374 us
  waiting for transfers between devices  158 us (41%)
  local copies, waits for them, and re-layouts  62.6 us (16%)
  blocking collectives  58.6 us (15%)
  matrix products  34 us (9%)
  starting transfers between devices  27.3 us (7%)
  other arithmetic  18.4 us (5%)
  between operations  15.6 us (4%)
    reduce_scatter x1, waiting for transfers between devices, body(): lax.psum_scatter(partial_sum, ('seq', 'fsdp'), scatter_dimension=0, tiled...  123 us
    all_to_all x1, blocking collectives, body(): lax.all_to_all(query_send, 'seq', split_axis=1, concat_axis=1, tiled=True)  58.6 us
    unnamed x144, local copies, waits for them, and re-layouts  18.8 us
    all_to_all x1, waiting for transfers between devices, body(): lax.all_to_all(grad_send, 'seq', split_axis=1, concat_axis=1, tiled=True)  11.6 us
    gather x4, local copies, waits for them, and re-layouts, to_slots(): jnp.take(rows, source.reshape(-1), axis=0)  10.4 us
    all_to_all x1, starting transfers between devices, body(): lax.all_to_all(key_send, 'seq', split_axis=1, concat_axis=1, tiled=True)  9.28 us
    all_to_all x1, waiting for transfers between devices, body(): lax.all_to_all(value_back, 'seq', split_axis=1, concat_axis=1, tiled=True)  8.87 us
    slice x5, local copies, waits for them, and re-layouts, attend(): q_item = query_in[:, :, item_index, :].reshape(slot_count, group, HD)  8.31 us
  transfers between devices with their start and end apart: 7, of which 6 were waited for; matrix products, arithmetic and copies ran while one was open for 23% of the time, Pallas kernels for 0%

commit v1 on v0

v1 whole, which is shorter than its diff:
```python
import functools
import math

import jax
import jax.numpy as jnp
from jax import lax
from jax.experimental import pallas as pl
from jax.experimental.pallas import tpu as pltpu
from jax.sharding import PartitionSpec as P

KVH = 4
HD = 128


SCORE_NEG = -1e30
EWC_LAMBDA = 4.0


def round_plan(starts, owner_list, lane_count, rounds):
    round_ids = jnp.arange(rounds, dtype=jnp.int32)
    start_rounds = starts // lane_count
    doc_of = jnp.sum((start_rounds[None, :] <= round_ids[:, None]).astype(jnp.int32), axis=1) - 1
    doc_ids = jnp.arange(starts.shape[0], dtype=jnp.int32)
    onehot = (doc_of[:, None] == doc_ids[None, :]).astype(jnp.int32)
    owner_of = jnp.sum(onehot * owner_list[None, :], axis=1)
    earlier = (owner_of[:, None] == owner_of[None, :]) & (round_ids[None, :] < round_ids[:, None])
    rank_of = jnp.sum(earlier.astype(jnp.int32), axis=1)
    return (doc_of, owner_of, rank_of)


def slot_rounds(owner_of, rank_of, lane_count, capacity):
    lane_ids = jnp.arange(lane_count, dtype=jnp.int32)
    slot_ids = jnp.arange(capacity, dtype=jnp.int32)
    round_ids = jnp.arange(owner_of.shape[0], dtype=jnp.int32)
    match = (owner_of[None, None, :] == lane_ids[None, :, None]) & (
        rank_of[None, None, :] == slot_ids[:, None, None]
    )
    source = jnp.sum(match.astype(jnp.int32) * round_ids[None, None, :], axis=2)
    filled = jnp.any(match, axis=2)
    return (source, filled)


def attend_kernel(lanes, capacity, q_ref, g_ref, kv_ref, vis_ref, dq_ref, dkv_ref):
    head = pl.program_id(0)
    slots = lanes * capacity
    scale = 1.0 / math.sqrt(HD)
    slot = lax.broadcasted_iota(jnp.int32, (slots, 1), 0)
    wanted = ((slot % lanes) * KVH + head) * capacity + slot // lanes
    columns = lax.broadcasted_iota(jnp.int32, (slots, slots * KVH), 1)
    pick = jnp.where(columns == wanted, 1.0, 0.0).astype(jnp.bfloat16)

    def dot(a, b, ca, cb):
        return lax.dot_general(
            a, b, (((ca,), (cb,)), ((), ())), preferred_element_type=jnp.float32
        )

    q_all = dot(pick, q_ref[...], 1, 0).astype(jnp.bfloat16)
    g_all = dot(pick, g_ref[...], 1, 0).astype(jnp.bfloat16)
    kv = dot(pick, kv_ref[...], 1, 0).astype(jnp.bfloat16)
    keys, values = kv[:, :HD], kv[:, HD:]
    visible = vis_ref[...] > 0.0
    key_sum = jnp.zeros((slots, HD), jnp.float32)
    value_sum = jnp.zeros((slots, HD), jnp.float32)
    for at in range(q_all.shape[1] // HD):
        q = q_all[:, at * HD : (at + 1) * HD]
        g = g_all[:, at * HD : (at + 1) * HD]
        masked = jnp.where(visible, dot(q, keys, 1, 1) * scale, SCORE_NEG)
        peak = jnp.max(masked, axis=1, keepdims=True)
        probs = jnp.where(visible, jnp.exp(masked - peak), 0.0)
        totals = jnp.sum(probs, axis=1, keepdims=True)
        probs = probs * (1.0 / jnp.where(totals > 0.0, totals, 1.0))
        probs_b = probs.astype(jnp.bfloat16)
        attn_out = dot(probs_b, values, 1, 0).astype(jnp.bfloat16)
        delta = jnp.sum(
            g.astype(jnp.float32) * attn_out.astype(jnp.float32), axis=1, keepdims=True
        )
        dprobs = dot(g, values, 1, 1)
        dscores = (probs * (dprobs - delta) * scale).astype(jnp.bfloat16)
        dq_ref[:, at * HD : (at + 1) * HD] = dot(dscores, keys, 1, 0).astype(jnp.bfloat16)
        key_sum = key_sum + dot(dscores, q, 0, 0)
        value_sum = value_sum + dot(probs_b, g, 0, 0)
    both = jnp.concatenate([key_sum, value_sum], axis=1).astype(jnp.bfloat16)
    placed = dot(pick, both, 0, 0).astype(jnp.bfloat16)

    @pl.when(head == 0)
    def _():
        dkv_ref[...] = placed

    @pl.when(head > 0)
    def _():
        dkv_ref[...] = dkv_ref[...] + placed


def attend(query_in, grad_in, kv_in, visible, lanes, capacity):
    slots = lanes * capacity
    rows, width = query_in.shape
    whole = lambda h: (0, 0)
    flops = 2 * slots * slots * width * KVH * 6 + 4 * rows * slots * width * KVH
    return pl.pallas_call(
        functools.partial(attend_kernel, lanes, capacity),
        grid=(KVH,),
        in_specs=[
            pl.BlockSpec((rows, width), whole),
            pl.BlockSpec((rows, width), whole),
            pl.BlockSpec((rows, 2 * HD), whole),
            pl.BlockSpec((slots, slots), whole),
        ],
        out_specs=[
            pl.BlockSpec((slots, width), lambda h: (0, h)),
            pl.BlockSpec((rows, 2 * HD), whole),
        ],
        out_shape=[
            jax.ShapeDtypeStruct((slots, width * KVH), jnp.bfloat16),
            jax.ShapeDtypeStruct((rows, 2 * HD), jnp.bfloat16),
        ],
        compiler_params=pltpu.CompilerParams(vmem_limit_bytes=40 * 1024 * 1024),
        cost_estimate=pl.CostEstimate(
            flops=flops,
            bytes_accessed=6 * rows * width,
            transcendentals=slots * slots * width * KVH // HD,
        ),
    )(query_in, grad_in, kv_in, visible)


def fetch_weight(value_weight):
    return lax.all_gather(value_weight, ("seq", "fsdp"), axis=0, tiled=True)


def body(inputs, queries, rotated_keys, out_grad, value_weight, fisher, anchor, doc_starts, owners):
    lane_count = lax.axis_size("seq")
    own_lane = lax.axis_index("seq")
    rounds = inputs.shape[1]
    capacity = 3 * rounds // (2 * lane_count)
    token_rows = inputs.reshape(rounds, inputs.shape[3])
    query_rows = queries.reshape(rounds, queries.shape[3])
    key_rows = rotated_keys.reshape(rounds, rotated_keys.shape[3])
    grad_rows = out_grad.reshape(rounds, out_grad.shape[3])
    doc_of, owner_of, rank_of = round_plan(doc_starts[0], owners[0], lane_count, rounds)
    source, filled = slot_rounds(owner_of, rank_of, lane_count, capacity)

    per_lane = KVH * capacity
    round_row = (owner_of[None, :] * KVH + jnp.arange(KVH, dtype=jnp.int32)[:, None]) * capacity
    round_row = (round_row + rank_of[None, :]).reshape(-1)
    row_ids = jnp.arange(lane_count * per_lane, dtype=jnp.int32)
    select = (row_ids[:, None] == round_row[None, :]).astype(jnp.bfloat16)

    def stacked(rows):
        width = rows.shape[1] // KVH
        return jnp.concatenate([rows[:, h * width : (h + 1) * width] for h in range(KVH)], axis=0)

    def exchange(rows):
        parts = rows.reshape(lane_count, per_lane, -1)
        moved = lax.all_to_all(parts, "seq", split_axis=0, concat_axis=0, tiled=True)
        return moved.reshape(lane_count * per_lane, -1)

    def to_owners(rows):
        return exchange(
            jnp.dot(select, rows, preferred_element_type=jnp.float32).astype(jnp.bfloat16)
        )

    full_weight = fetch_weight(value_weight)
    query_in = to_owners(stacked(query_rows))
    grad_in = to_owners(stacked(grad_rows))
    my_rounds = lax.dynamic_index_in_dim(source, own_lane, 1, keepdims=False)
    my_filled = lax.dynamic_index_in_dim(filled, own_lane, 1, keepdims=False)
    lane_ids = jnp.arange(lane_count, dtype=jnp.int32)
    slot_pos = (my_rounds[:, None] * lane_count + lane_ids[None, :]).reshape(-1)
    round_doc = jnp.where(my_filled, jnp.take(doc_of, my_rounds), -1)
    slot_doc = jnp.broadcast_to(round_doc[:, None], (capacity, lane_count)).reshape(-1)
    slot_live = jnp.broadcast_to(my_filled[:, None], (capacity, lane_count)).reshape(-1)
    visible = (slot_doc[:, None] == slot_doc[None, :]) & (slot_pos[None, :] <= slot_pos[:, None])
    visible = visible & slot_live[:, None] & slot_live[None, :]
    value_rows = jnp.dot(token_rows, full_weight, preferred_element_type=jnp.float32).astype(
        jnp.bfloat16
    )
    kv_in = to_owners(jnp.concatenate([stacked(key_rows), stacked(value_rows)], axis=1))
    kv_in, grad_in, later_rows = lax.optimization_barrier((kv_in, grad_in, token_rows))
    token_cols = lax.all_to_all(
        later_rows.reshape(rounds, lane_count, -1), "seq", split_axis=1, concat_axis=1, tiled=True
    )
    query_back, kv_back = attend(
        query_in, grad_in, kv_in, visible.astype(jnp.float32), lane_count, capacity
    )
    home = lax.dot_general(
        select, exchange(kv_back), (((0,), (0,)), ((), ())), preferred_element_type=jnp.float32
    ).astype(jnp.bfloat16)
    pieces = [home[h * rounds : (h + 1) * rounds] for h in range(KVH)]
    key_home = jnp.concatenate([piece[:, :HD] for piece in pieces], axis=1)
    value_home = jnp.concatenate([piece[:, HD:] for piece in pieces], axis=1)
    input_grad = jnp.einsum(
        "rk,dk->rd", value_home, full_weight, preferred_element_type=jnp.float32
    ).astype(jnp.bfloat16)
    all_values = lax.all_gather(value_home, "seq", axis=0, tiled=False)
    partial_sum = jnp.einsum(
        "rld,lrk->dk", token_cols, all_values, preferred_element_type=jnp.float32
    )
    summed = lax.psum_scatter(partial_sum, "fsdp", scatter_dimension=0, tiled=True)
    tokens_total = rounds * lane_count * lax.axis_size("fsdp")
    grad_scale = 1.0 / math.sqrt(tokens_total)
    ewc_grad = summed * grad_scale + EWC_LAMBDA * fisher * (
        value_weight.astype(jnp.float32) - anchor
    )
    query_out = query_back.reshape(1, 1, capacity, lane_count, -1)
    return (
        query_out,
        key_home.reshape(1, rounds, 1, -1),
        input_grad.reshape(1, rounds, 1, -1),
        ewc_grad,
    )


def solution(mesh):
    return jax.shard_map(
        body,
        mesh=mesh,
        in_specs=(
            P("fsdp", None, "seq", None),
            P("fsdp", None, "seq", None),
            P("fsdp", None, "seq", None),
            P("fsdp", None, "seq", None),
            P(("seq", "fsdp"), None),
            P(("seq", "fsdp"), None),
            P(("seq", "fsdp"), None),
            P("fsdp", None),
            P("fsdp", None),
        ),
        out_specs=(
            P("fsdp", "seq", None, None, None),
            P("fsdp", None, "seq", None),
            P("fsdp", None, "seq", None),
            P(("seq", "fsdp"), None),
        ),
        check_vma=False,
    )
```

time: 381 us -> 270 us (0.71); the launches traced: 374 us -> 269 us
  local copies, waits for them, and re-layouts: 62.6 us -> 12.4 us
  blocking collectives: 58.6 us -> 21.2 us
  Pallas kernels: 0 us -> 26.9 us
  matrix products: 34 us -> 15.1 us
  other arithmetic: 18.4 us -> 9.83 us
  starting transfers between devices: 27.3 us -> 18.9 us
  waiting for transfers between devices: 158 us -> 151 us
    reduce_scatter x1, waiting for transfers between devices: 123 us -> 8.19 us  [body(): lax.psum_scatter(partial_sum, 'fsdp', scatter_dimension=0, tiled=True)]
    all_gather x1, waiting for transfers between devices: 0.01 us -> 65.8 us  [fetch_weight(): return lax.all_gather(value_weight, ('seq', 'fsdp'), axis=0, tiled=True)]
    all_gather x0 -> x1, waiting for transfers between devices: none -> 45.2 us  [body(): all_values = lax.all_gather(value_home, 'seq', axis=0, tiled=False)]
    all_to_all x1, blocking collectives: 58.6 us -> 21.2 us  [exchange(): lax.all_to_all(parts, 'seq', split_axis=0, concat_axis=0, tiled=True)]
    pallas_call x0 -> x1, Pallas kernels: none -> 26.9 us  [attend(): pl.pallas_call(functools.partial(attend_kernel, lanes, capacity), grid=(K...]
    unnamed x144 -> x25, local copies, waits for them, and re-layouts: 18.8 us -> 1.75 us
    slice x20 -> x5, local copies, waits for them, and re-layouts: 14.6 us -> 1.44 us  [the longest x4 1.4 us: stacked(): rows[:, h * width:(h + 1) * width]]
    gather x6 -> x0, local copies, waits for them, and re-layouts: 12.2 us -> none  [the longest x4 10.4 us: to_slots(): jnp.take(rows, source.reshape(-1), axis=0)]
  transfers between devices with their start and end apart: 7 -> 7, of which waited for: 6 -> 5; matrix products, arithmetic and copies ran while one was open for 23% -> 12% of each run, Pallas kernels for 0% -> 0%
where the time goes in v1:
time: 270 us; the launch traced here: 269 us
  waiting for transfers between devices  151 us (56%)
  Pallas kernels  26.9 us (10%)
  blocking collectives  21.2 us (8%)
  starting transfers between devices  18.9 us (7%)
  matrix products  15.1 us (6%)
  between operations  14 us (5%)
  local copies, waits for them, and re-layouts  12.4 us (5%)
  other arithmetic  9.83 us (4%)
    all_gather x1, waiting for transfers between devices, fetch_weight(): return lax.all_gather(value_weight, ('seq', 'fsdp'), axis=0, tiled=True)  65.8 us
    all_gather x1, waiting for transfers between devices, body(): all_values = lax.all_gather(value_home, 'seq', axis=0, tiled=False)  45.2 us
    all_to_all x3, waiting for transfers between devices, exchange(): lax.all_to_all(parts, 'seq', split_axis=0, concat_axis=0, tiled=True)  31 us
    pallas_call x1, Pallas kernels, attend(): pl.pallas_call(functools.partial(attend_kernel, lanes, capacity), grid=(K...  26.9 us
    all_to_all x1, blocking collectives, exchange(): lax.all_to_all(parts, 'seq', split_axis=0, concat_axis=0, tiled=True)  21.2 us
    all_to_all x3, starting transfers between devices, exchange(): lax.all_to_all(parts, 'seq', split_axis=0, concat_axis=0, tiled=True)  15.1 us
    reduce_scatter x1, waiting for transfers between devices, body(): lax.psum_scatter(partial_sum, 'fsdp', scatter_dimension=0, tiled=True)  8.19 us
    dot_general x3, matrix products, to_owners(): jnp.dot(select, rows, preferred_element_type=jnp.float32)  5.44 us
  transfers between devices with their start and end apart: 7, of which 5 were waited for; matrix products, arithmetic and copies ran while one was open for 12% of the time, Pallas kernels for 0%

profile of v1, /device:TPU:0, one launch (start us, length us, event | category | flops | bytes accessed | tf_op | source)
XLA Modules:
  0.0 269.3 jit_solution(5268772357665216949)
XLA Ops:
  10.9 2.1 convolution_convert_fusion.1
  13.0 7.5 %all-to-all-start.2 = ((bf16[16,48,1024]{2,1,0:T(8,128)(2,1)}), bf16[16,48,1024]{2,1,0:T(8,128)(2,1)S(1)}, u32[]{:S(2)}, u32[]{:S(2)}) async-start(bf16[16,48,1024]{2,1,0:T(8,128)(2,1)} %bitcast.41), calls=%async_computation.2 | async-start | bytes 3145728 | tf_op jit(solution)/shard_map/all_to_all | solution.py:153
  20.6 65.8 %all-gather.4.cloned.1.call-done = bf16[4096,512]{1,0:T(8,128)(2,1)} async-done(((bf16[128,512]{1,0:T(8,128)(2,1)}), bf16[4096,512]{1,0:T(8,128)(2,1)}) %all-gather.4.cloned.1.call-update) | async-done | bytes 4194320 | tf_op jit(solution)/shard_map/all_gather | solution.py:126
  86.4 3.0 %convolution_convert_fusion.3 = bf16[128,512]{1,0:T(8,128)(2,1)S(1)} fusion(bf16[4096,512]{1,0:T(8,128)(2,1)} %all-gather.4.cloned.1.call-done, bf16[1,128,1,4096]{3,1,2,0:T(8,128)(2,1)S(1)} %copy-done.1), kind=kOutput, calls=%fused_computation.11 | convolution fusion | flops 536936448 | bytes 5373952 | tf_op jit(solution)/shard_map/dot_general | solution.py:173
  90.6 3.9 %all-to-all-start.1 = ((bf16[16,48,256]{2,1,0:T(8,128)(2,1)}), bf16[16,48,256]{2,1,0:T(8,128)(2,1)S(1)}, u32[]{:S(2)}, u32[]{:S(2)}) async-start(bf16[16,48,256]{2,1,0:T(8,128)(2,1)} %bitcast.8), calls=%async_computation.1 | async-start | bytes 786432 | tf_op jit(solution)/shard_map/all_to_all | solution.py:153
  94.6 2.1 convolution_convert_fusion.2
  96.8 9.9 %all-to-all-done.1 = bf16[16,48,256]{2,1,0:T(8,128)(2,1)S(1)} async-done(((bf16[16,48,256]{2,1,0:T(8,128)(2,1)}), bf16[16,48,256]{2,1,0:T(8,128)(2,1)S(1)}, u32[]{:S(2)}, u32[]{:S(2)}) %all-to-all-start.1) | async-done | bytes 393248 | tf_op jit(solution)/shard_map/all_to_all | solution.py:153
  106.7 3.7 %all-to-all-start = ((bf16[16,48,1024]{2,1,0:T(8,128)(2,1)}), bf16[16,48,1024]{2,1,0:T(8,128)(2,1)S(1)}, u32[]{:S(2)}, u32[]{:S(2)}) async-start(bf16[16,48,1024]{2,1,0:T(8,128)(2,1)} %bitcast.40), calls=%async_computation | async-start | bytes 3145728 | tf_op jit(solution)/shard_map/all_to_all | solution.py:153
  111.7 1.3 and.58
  114.8 1.3 gather_fusion
  116.1 1.3 copy.23
  117.4 1.4 select_reduce_fusion.1
  119.8 1.5 and_convert_fusion.vis_ref
  121.3 21.0 %all-to-all-done = bf16[16,48,1024]{2,1,0:T(8,128)(2,1)S(1)} async-done(((bf16[16,48,1024]{2,1,0:T(8,128)(2,1)}), bf16[16,48,1024]{2,1,0:T(8,128)(2,1)S(1)}, u32[]{:S(2)}, u32[]{:S(2)}) %all-to-all-start) | async-done | bytes 1572896 | tf_op jit(solution)/shard_map/all_to_all | solution.py:153
  143.3 26.9 %shard_map.120 = (bf16[192,4096]{1,0:T(8,128)(2,1)}, bf16[768,256]{1,0:T(8,128)(2,1)S(1)}) custom-call(bf16[768,1024]{1,0:T(8,128)(2,1)S(1)} %bitcast.35, bf16[768,1024]{1,0:T(8,128)(2,1)S(1)} %bitcast.34, bf16[768,256]{1,0:T(8,128)(2,1)S(1)} %bitcast.36, f32[192,192]{1,0:T(8,128)S(1)} %copy-done), custom_call_target="tpu_custom_call" | custom-call | flops 4227858432 | bytes 4718592 | tf_op jit(solution)/shard_map/pallas_call | solution.py:99
  170.2 21.2 %all_to_all.25 = bf16[16,48,256]{2,1,0:T(8,128)(2,1)S(1)} all-to-all(bf16[16,48,256]{2,1,0:T(8,128)(2,1)S(1)} %bitcast.37), channel_id=1, replica_groups=mesh['seq'=16,'fsdp'=2] {'seq'}, dimensions={0} | all-to-all | bytes 786432 | tf_op jit(solution)/shard_map/all_to_all | solution.py:153
  192.7 1.3 copy.24
  194.0 3.7 %all-to-all-start.4 = ((bf16[128,16,256]{0,2,1:T(8,128)(2,1)}), bf16[128,16,256]{0,2,1:T(8,128)(2,1)S(1)}, u32[]{:S(2)}, u32[]{:S(2)}) async-start(bf16[128,16,256]{0,2,1:T(8,128)(2,1)} %bitcast.19), calls=%async_computation.4 | async-start | bytes 2097152 | tf_op jit(solution)/shard_map/all_to_all | solution.py:178
  197.7 45.2 %all-gather.6.cloned.1.call-done = bf16[2048,512]{0,1:T(8,128)(2,1)} async-done(((bf16[128,512]{0,1:T(8,128)(2,1)}), bf16[2048,512]{0,1:T(8,128)(2,1)}) %all-gather.6.cloned.1.call-update) | async-done | bytes 2097168 | tf_op jit(solution)/shard_map/all_gather | solution.py:193
  242.9 2.9 %copy.27 = bf16[2048,512]{1,0:T(8,128)(2,1)S(1)} copy(bf16[2048,512]{0,1:T(8,128)(2,1)} %all-gather.6.cloned.1.call-done) | data formatting | bytes 4194304 | tf_op jit(solution)/shard_map/all_gather | solution.py:193
  245.8 1.5 convolution_bitcast_fusion
  248.1 4.7 %fusion = bf16[1,128,1,4096]{3,1,2,0:T(8,128)(2,1)} fusion(bf16[4096,512]{1,0:T(8,128)(2,1)} %all-gather.4.cloned.1.call-done, bf16[128,128]{0,1:T(8,128)(2,1)S(1)} %get-tuple-element.41, bf16[128,128]{0,1:T(8,128)(2,1)S(1)} %get-tuple-element.42, bf16[128,128]{0,1:T(8,128)(2,1)S(1)} %get-tuple-element.43, bf16[128,128]{0,1:T(8,128)(2,1)S(1)} %get-tuple-element.40), kind=kOutput, calls=%fused_computation.2 | convolution fusion | flops 537919488 | bytes 5373952 | tf_op jit(solution)/shard_map/rk,dk->rd/dot_general | solution.py:190
  252.8 8.2 %reduce-scatter.2.cloned.1.call-done = f32[128,512]{1,0:T(8,128)} async-done(((f32[256,512]{1,0:T(8,128)}), f32[128,512]{1,0:T(8,128)}) %reduce-scatter.2.cloned.1.call-update) | async-done | bytes 262160 | tf_op jit(solution)/shard_map/reduce_scatter | solution.py:197
  261.0 1.7 multiply_add_fusion
  (61 shorter events, 11.9 us)
Async XLA Ops:
  7.2 79.2 %all-gather.4.cloned.1.call-start = ((), (), s32[]{:S(2)}) async-start(), calls=%async_computation.6 | async-start | bytes 4325376 | tf_op jit(solution)/shard_map/all_gather | solution.py:126
  9.6 85.0 %copy-start.10 = (s32[512]{0:T(512)}, s32[512]{0:T(512)S(1)}, u32[]{:S(2)}) copy-start(s32[512]{0:T(512)S(1)} %add_bitcast_fusion) | copy-start | bytes 6148
  13.0 7.5 %copy-start.7 = (bf16[1,128,1,512]{3,1,2,0:T(8,128)(2,1)S(1)}, bf16[1,128,1,512]{3,1,2,0:T(8,128)(2,1)}, u32[]{:S(2)}) copy-start(bf16[1,128,1,512]{3,1,2,0:T(8,128)(2,1)} %param.11) | copy-start | bytes 393220
  13.0 73.4 %copy-start.1 = (bf16[1,128,1,4096]{3,1,2,0:T(8,128)(2,1)S(1)}, bf16[1,128,1,4096]{3,1,2,0:T(8,128)(2,1)}, u32[]{:S(2)}) copy-start(bf16[1,128,1,4096]{3,1,2,0:T(8,128)(2,1)} %param.9) | copy-start | bytes 3145732
  13.0 77.6 %all-to-all-start.2 = ((bf16[16,48,1024]{2,1,0:T(8,128)(2,1)}), bf16[16,48,1024]{2,1,0:T(8,128)(2,1)S(1)}, u32[]{:S(2)}, u32[]{:S(2)}) async-start(bf16[16,48,1024]{2,1,0:T(8,128)(2,1)} %bitcast.41), calls=%async_computation.2 | async-start | bytes 3145728 | tf_op jit(solution)/shard_map/all_to_all | solution.py:153
  89.4 5.2 %copy-start.3 = (bf16[1,128,1,4096]{3,1,2,0:T(8,128)(2,1)S(1)}, bf16[1,128,1,4096]{3,1,2,0:T(8,128)(2,1)}, u32[]{:S(2)}) copy-start(bf16[1,128,1,4096]{3,1,2,0:T(8,128)(2,1)} %param.10) | copy-start | bytes 3145732
  90.6 16.1 %all-to-all-start.1 = ((bf16[16,48,256]{2,1,0:T(8,128)(2,1)}), bf16[16,48,256]{2,1,0:T(8,128)(2,1)S(1)}, u32[]{:S(2)}, u32[]{:S(2)}) async-start(bf16[16,48,256]{2,1,0:T(8,128)(2,1)} %bitcast.8), calls=%async_computation.1 | async-start | bytes 786432 | tf_op jit(solution)/shard_map/all_to_all | solution.py:153
  106.7 35.6 %all-to-all-start = ((bf16[16,48,1024]{2,1,0:T(8,128)(2,1)}), bf16[16,48,1024]{2,1,0:T(8,128)(2,1)S(1)}, u32[]{:S(2)}, u32[]{:S(2)}) async-start(bf16[16,48,1024]{2,1,0:T(8,128)(2,1)} %bitcast.40), calls=%async_computation | async-start | bytes 3145728 | tf_op jit(solution)/shard_map/all_to_all | solution.py:153
  110.5 132.5 %all-gather.6.cloned.1.call-start = ((), (), s32[]{:S(2)}) async-start(), calls=%async_computation.8 | async-start | bytes 2228224 | tf_op jit(solution)/shard_map/all_gather | solution.py:193
  110.5 1.2 copy-start.8
  110.5 1.2 copy-start.9
  142.4 0.9 copy-start
  143.3 48.1 %copy-start.11 = (s32[512]{0:T(512)S(1)}, s32[512]{0:T(512)}, u32[]{:S(2)}) copy-start(s32[512]{0:T(512)} %copy-done.10) | copy-start | bytes 6148
  170.2 22.5 %copy-start.2 = (bf16[1,128,1,4096]{3,1,2,0:T(8,128)(2,1)S(1)}, bf16[1,128,1,4096]{3,1,2,0:T(8,128)(2,1)}, u32[]{:S(2)}) copy-start(bf16[1,128,1,4096]{3,1,2,0:T(8,128)(2,1)} %param.9) | copy-start | bytes 3145732
  194.0 51.8 %all-to-all-start.4 = ((bf16[128,16,256]{0,2,1:T(8,128)(2,1)}), bf16[128,16,256]{0,2,1:T(8,128)(2,1)S(1)}, u32[]{:S(2)}, u32[]{:S(2)}) async-start(bf16[128,16,256]{0,2,1:T(8,128)(2,1)} %bitcast.19), calls=%async_computation.4 | async-start | bytes 2097152 | tf_op jit(solution)/shard_map/all_to_all | solution.py:178
  197.6 63.4 %reduce-scatter.2.cloned.1.call-start = ((), (), s32[]{:S(2)}) async-start(), calls=%async_computation.7 | async-start | bytes 786432 | tf_op jit(solution)/shard_map/reduce_scatter | solution.py:197
  248.1 12.9 %copy-start.4 = (bf16[128,512]{1,0:T(8,128)(2,1)S(1)}, bf16[128,512]{1,0:T(8,128)(2,1)}, u32[]{:S(2)}) copy-start(bf16[128,512]{1,0:T(8,128)(2,1)} %param.13) | copy-start | bytes 393220
  248.1 12.9 %copy-start.5 = (f32[128,512]{1,0:T(8,128)S(1)}, f32[128,512]{1,0:T(8,128)}, u32[]{:S(2)}) copy-start(f32[128,512]{1,0:T(8,128)} %param.15) | copy-start | bytes 786436
  248.1 12.9 %copy-start.6 = (f32[128,512]{1,0:T(8,128)S(1)}, f32[128,512]{1,0:T(8,128)}, u32[]{:S(2)}) copy-start(f32[128,512]{1,0:T(8,128)} %param.14) | copy-start | bytes 786436
Sparse Core Ops, SparseCore 0:
  10.9 75.4 all-gather.3
  192.8 50.1 all-gather.5
  247.5 13.5 reduce-scatter.1

commit v2 on v1

--- a/solution.py
+++ b/solution.py
@@ -122,6 +122,52 @@
     )(query_in, grad_in, kv_in, visible)
 
 
+def lane_products(token_cols, value_home, lane_count, own_lane):
+    steps = []
+    step = lane_count // 2
+    while step >= 1:
+        steps.append(step)
+        step //= 2
+    offsets = [0]
+    for step in steps:
+        offsets = offsets + [at ^ step for at in offsets]
+    ordered = jnp.concatenate(
+        [lax.dynamic_slice_in_dim(token_cols, own_lane ^ at, 1, 0) for at in offsets], axis=0
+    )
+
+    def product(first, values):
+        tokens = ordered[first : first + values.shape[0]].reshape(-1, ordered.shape[2])
+        return lax.dot_general(
+            tokens,
+            values.reshape(-1, values.shape[2]),
+            (((0,), (0,)), ((), ())),
+            preferred_element_type=jnp.float32,
+        )
+
+    held = value_home[None]
+    total = product(0, held)
+    for step in steps:
+        pairs = [(lane, lane ^ step) for lane in range(lane_count)]
+        arrived = lax.ppermute(held, "seq", pairs)
+        total = total + product(held.shape[0], arrived)
+        if step > 1:
+            held = jnp.concatenate([held, arrived], axis=0)
+    return total
+
+
+def sum_rows(partial_sum):
+    count = lax.axis_size("fsdp")
+    own = lax.axis_index("fsdp")
+    rows = partial_sum.shape[0] // count
+    total = lax.dynamic_slice_in_dim(partial_sum, own * rows, rows, 0)
+    for shift in range(1, count):
+        target = (own + shift) % count
+        part = lax.dynamic_slice_in_dim(partial_sum, target * rows, rows, 0)
+        pairs = [(at, (at + shift) % count) for at in range(count)]
+        total = total + lax.ppermute(part, "fsdp", pairs)
+    return total
+
+
 def fetch_weight(value_weight):
     return lax.all_gather(value_weight, ("seq", "fsdp"), axis=0, tiled=True)
 
@@ -170,17 +216,23 @@
     slot_live = jnp.broadcast_to(my_filled[:, None], (capacity, lane_count)).reshape(-1)
     visible = (slot_doc[:, None] == slot_doc[None, :]) & (slot_pos[None, :] <= slot_pos[:, None])
     visible = visible & slot_live[:, None] & slot_live[None, :]
-    value_rows = jnp.dot(token_rows, full_weight, preferred_element_type=jnp.float32).astype(
+    value_tokens, query_in, grad_in = lax.optimization_barrier((token_rows, query_in, grad_in))
+    value_rows = jnp.dot(value_tokens, full_weight, preferred_element_type=jnp.float32).astype(
         jnp.bfloat16
     )
     kv_in = to_owners(jnp.concatenate([stacked(key_rows), stacked(value_rows)], axis=1))
     kv_in, grad_in, later_rows = lax.optimization_barrier((kv_in, grad_in, token_rows))
     token_cols = lax.all_to_all(
-        later_rows.reshape(rounds, lane_count, -1), "seq", split_axis=1, concat_axis=1, tiled=True
+        later_rows.reshape(rounds, lane_count, -1).transpose(1, 0, 2),
+        "seq",
+        split_axis=0,
+        concat_axis=0,
+        tiled=True,
     )
     query_back, kv_back = attend(
         query_in, grad_in, kv_in, visible.astype(jnp.float32), lane_count, capacity
     )
+    kv_back, token_cols = lax.optimization_barrier((kv_back, token_cols))
     home = lax.dot_general(
         select, exchange(kv_back), (((0,), (0,)), ((), ())), preferred_element_type=jnp.float32
     ).astype(jnp.bfloat16)
@@ -190,11 +242,8 @@
     input_grad = jnp.einsum(
         "rk,dk->rd", value_home, full_weight, preferred_element_type=jnp.float32
     ).astype(jnp.bfloat16)
-    all_values = lax.all_gather(value_home, "seq", axis=0, tiled=False)
-    partial_sum = jnp.einsum(
-        "rld,lrk->dk", token_cols, all_values, preferred_element_type=jnp.float32
-    )
-    summed = lax.psum_scatter(partial_sum, "fsdp", scatter_dimension=0, tiled=True)
+    partial_sum = lane_products(token_cols, value_home, lane_count, own_lane)
+    summed = sum_rows(partial_sum)
     tokens_total = rounds * lane_count * lax.axis_size("fsdp")
     grad_scale = 1.0 / math.sqrt(tokens_total)
     ewc_grad = summed * grad_scale + EWC_LAMBDA * fisher * (

time: 270 us -> 256 us (0.948)
  waiting for transfers between devices: 151 us -> 105 us
  blocking collectives: 21.2 us -> 38.7 us
  starting transfers between devices: 18.9 us -> 28.2 us
  local copies, waits for them, and re-layouts: 12.4 us -> 18 us
    all_gather x1, waiting for transfers between devices: 65.8 us -> 0.01 us  [fetch_weight(): return lax.all_gather(value_weight, ('seq', 'fsdp'), axis=0, tiled=True)]
    all_gather x1 -> x0, waiting for transfers between devices: 45.2 us -> none  [body(): all_values = lax.all_gather(value_home, 'seq', axis=0, tiled=False)]
    all_to_all x3 -> x2, waiting for transfers between devices: 31 us -> 76.2 us  [exchange(): lax.all_to_all(parts, 'seq', split_axis=0, concat_axis=0, tiled=True)]
    ppermute x0 -> x5, waiting for transfers between devices: none -> 28.3 us  [the longest x4 23.8 us: lane_products(): arrived = lax.ppermute(held, 'seq', pairs)]
    all_to_all x1 -> x2, blocking collectives: 21.2 us -> 38.7 us  [exchange(): lax.all_to_all(parts, 'seq', split_axis=0, concat_axis=0, tiled=True)]
    reduce_scatter x1 -> x0, waiting for transfers between devices: 8.19 us -> none  [body(): lax.psum_scatter(partial_sum, 'fsdp', scatter_dimension=0, tiled=True)]
    unnamed x25 -> x28, local copies, waits for them, and re-layouts: 1.75 us -> 8.12 us
    ppermute x0 -> x5, starting transfers between devices: none -> 5.15 us  [the longest x4 3.31 us: lane_products(): arrived = lax.ppermute(held, 'seq', pairs)]
  transfers between devices with their start and end apart: 7 -> 9, of which waited for: 5 -> 6; matrix products, arithmetic and copies ran while one was open for 12% -> 12% of each run, Pallas kernels for 0% -> 11%
where the time goes in v2:
time: 256 us; the launch traced here: 255 us
  waiting for transfers between devices  105 us (41%)
  blocking collectives  38.7 us (15%)
  starting transfers between devices  28.2 us (11%)
  Pallas kernels  26.9 us (11%)
  local copies, waits for them, and re-layouts  18 us (7%)
  matrix products  15.5 us (6%)
  between operations  14.4 us (6%)
  other arithmetic  8.19 us (3%)
    all_to_all x2, waiting for transfers between devices, exchange(): lax.all_to_all(parts, 'seq', split_axis=0, concat_axis=0, tiled=True)  76.2 us
    all_to_all x2, blocking collectives, exchange(): lax.all_to_all(parts, 'seq', split_axis=0, concat_axis=0, tiled=True)  38.7 us
    pallas_call x1, Pallas kernels, attend(): pl.pallas_call(functools.partial(attend_kernel, lanes, capacity), grid=(K...  26.9 us
    ppermute x4, waiting for transfers between devices, lane_products(): arrived = lax.ppermute(held, 'seq', pairs)  23.8 us
    all_to_all x2, starting transfers between devices, exchange(): lax.all_to_all(parts, 'seq', split_axis=0, concat_axis=0, tiled=True)  18.7 us
    unnamed x28, local copies, waits for them, and re-layouts  8.12 us
  transfers between devices with their start and end apart: 9, of which 6 were waited for; matrix products, arithmetic and copies ran while one was open for 12% of the time, Pallas kernels for 11%

profile of v2, /device:TPU:0, one launch (start us, length us, event | category | flops | bytes accessed | tf_op | source)
XLA Modules:
  0.0 255.2 jit_solution(3466548733787590199)
XLA Ops:
  10.9 2.1 convolution_convert_fusion.2
  13.0 7.5 %all-to-all-start = ((bf16[16,48,1024]{2,1,0:T(8,128)(2,1)}), bf16[16,48,1024]{2,1,0:T(8,128)(2,1)S(1)}, u32[]{:S(2)}, u32[]{:S(2)}) async-start(bf16[16,48,1024]{2,1,0:T(8,128)(2,1)} %bitcast.5), calls=%async_computation | async-start | bytes 3145728 | tf_op jit(solution)/shard_map/all_to_all | solution.py:199
  20.6 2.2 convolution_convert_fusion.1
  22.8 36.0 %all-to-all-done = bf16[16,48,1024]{2,1,0:T(8,128)(2,1)S(1)} async-done(((bf16[16,48,1024]{2,1,0:T(8,128)(2,1)}), bf16[16,48,1024]{2,1,0:T(8,128)(2,1)S(1)}, u32[]{:S(2)}, u32[]{:S(2)}) %all-to-all-start) | async-done | bytes 1572896 | tf_op jit(solution)/shard_map/all_to_all | solution.py:199
  58.8 11.2 %all-to-all-start.1 = ((bf16[16,48,1024]{2,1,0:T(8,128)(2,1)}), bf16[16,48,1024]{2,1,0:T(8,128)(2,1)S(1)}, u32[]{:S(2)}, u32[]{:S(2)}) async-start(bf16[16,48,1024]{2,1,0:T(8,128)(2,1)} %bitcast.58), calls=%async_computation.1 | async-start | bytes 3145728 | tf_op jit(solution)/shard_map/all_to_all | solution.py:199
  70.0 40.3 %all-to-all-done.1 = bf16[16,48,1024]{2,1,0:T(8,128)(2,1)S(1)} async-done(((bf16[16,48,1024]{2,1,0:T(8,128)(2,1)}), bf16[16,48,1024]{2,1,0:T(8,128)(2,1)S(1)}, u32[]{:S(2)}, u32[]{:S(2)}) %all-to-all-start.1) | async-done | bytes 1572896 | tf_op jit(solution)/shard_map/all_to_all | solution.py:199
  110.3 3.2 %convolution_convert_fusion.3 = bf16[128,512]{1,0:T(8,128)(2,1)S(1)} fusion(bf16[128,4096]{1,0:T(8,128)(2,1)} %bitcast.56, bf16[4096,512]{1,0:T(8,128)(2,1)} %all-gather.2.cloned.1.call-done), kind=kOutput, calls=%fused_computation.17 | convolution fusion | flops 536936448 | bytes 5373952 | tf_op jit(solution)/shard_map/dot_general | solution.py:220
  114.0 20.7 %all_to_all.25 = bf16[16,48,256]{2,1,0:T(8,128)(2,1)S(1)} all-to-all(bf16[16,48,256]{2,1,0:T(8,128)(2,1)S(1)} %bitcast.61), channel_id=1, replica_groups=mesh['seq'=16,'fsdp'=2] {'seq'}, dimensions={0} | all-to-all | bytes 786432 | tf_op jit(solution)/shard_map/all_to_all | solution.py:199
  134.7 2.3 copy.30
  136.9 4.3 %all-to-all-start.3 = ((bf16[16,128,256]{1,2,0:T(8,128)(2,1)}), bf16[16,128,256]{1,2,0:T(8,128)(2,1)}, u32[]{:S(2)}, u32[]{:S(2)}) async-start(bf16[16,128,256]{1,2,0:T(8,128)(2,1)} %bitcast.55), calls=%async_computation.3 | async-start | bytes 2097152 | tf_op jit(solution)/shard_map/all_to_all | solution.py:225
  144.3 1.3 copy.29
  146.6 1.4 select_reduce_fusion.1
  150.8 26.9 %shard_map.120 = (bf16[192,4096]{1,0:T(8,128)(2,1)}, bf16[768,256]{1,0:T(8,128)(2,1)S(1)}) custom-call(bf16[768,1024]{1,0:T(8,128)(2,1)S(1)} %bitcast.51, bf16[768,1024]{1,0:T(8,128)(2,1)S(1)} %bitcast.52, bf16[768,256]{1,0:T(8,128)(2,1)S(1)} %bitcast.53, f32[192,192]{1,0:T(8,128)S(1)} %and_convert_fusion.vis_ref), custom_call_target="tpu_custom_call" | custom-call | flops 4227858432 | bytes 4718592 | tf_op jit(solution)/shard_map/pallas_call | solution.py:99
  178.4 18.1 %all_to_all.26 = bf16[16,48,256]{2,1,0:T(8,128)(2,1)S(1)} all-to-all(bf16[16,48,256]{2,1,0:T(8,128)(2,1)} %bitcast.54), channel_id=1, replica_groups=mesh['seq'=16,'fsdp'=2] {'seq'}, dimensions={0} | all-to-all | bytes 786432 | tf_op jit(solution)/shard_map/all_to_all | solution.py:199
  197.1 1.8 collective-permute-start
  198.9 7.5 %collective-permute-done = bf16[1,128,512]{1,2,0:T(8,128)(2,1)S(1)} collective-permute-done((bf16[1,128,512]{1,2,0:T(8,128)(2,1)S(1)}, bf16[1,128,512]{1,2,0:T(8,128)(2,1)S(1)}, u32[]{:S(2)}, u32[]{:S(2)}) %collective-permute-start) | collective-permute-done | bytes 131104 | tf_op jit(solution)/shard_map/ppermute | solution.py:151
  206.5 7.6 %collective-permute-done.1 = bf16[2,128,512]{1,2,0:T(8,128)(2,1)S(1)} collective-permute-done((bf16[2,128,512]{1,2,0:T(8,128)(2,1)S(1)}, bf16[2,128,512]{1,2,0:T(8,128)(2,1)S(1)}, u32[]{:S(2)}, u32[]{:S(2)}) %collective-permute-start.1) | collective-permute-done | bytes 262176 | tf_op jit(solution)/shard_map/ppermute | solution.py:151
  214.2 1.4 collective-permute-start.2
  218.1 8.7 %collective-permute-done.2 = bf16[4,128,512]{1,2,0:T(8,128)(2,1)} collective-permute-done((bf16[4,128,512]{1,2,0:T(8,128)(2,1)S(1)}, bf16[4,128,512]{1,2,0:T(8,128)(2,1)}, u32[]{:S(2)}, u32[]{:S(2)}) %collective-permute-start.2) | collective-permute-done | bytes 524320 | tf_op jit(solution)/shard_map/ppermute | solution.py:151
  231.5 1.7 constant_dynamic-slice_fusion.6
  235.3 1.5 convolution_bitcast_fusion.1
  238.7 1.8 collective-permute-start.4
  240.6 2.5 fusion
  243.0 4.5 %collective-permute-done.4 = f32[128,512]{1,0:T(8,128)S(1)} collective-permute-done((f32[128,512]{1,0:T(8,128)S(1)}, f32[128,512]{1,0:T(8,128)S(1)}, u32[]{:S(2)}, u32[]{:S(2)}) %collective-permute-start.4) | collective-permute-done | bytes 262176 | tf_op jit(solution)/shard_map/ppermute | solution.py:167
  (75 shorter events, 24.3 us)
Async XLA Ops:
  7.2 103.2 %all-gather.2.cloned.1.call-start = ((), (), s32[]{:S(2)}) async-start(), calls=%async_computation.5 | async-start | bytes 4325376 | tf_op jit(solution)/shard_map/all_gather | solution.py:172
  9.6 104.0 %copy-start.8 = (s32[512]{0:T(512)}, s32[512]{0:T(512)S(1)}, u32[]{:S(2)}) copy-start(s32[512]{0:T(512)S(1)} %add_bitcast_fusion) | copy-start | bytes 6148
  13.0 7.5 %copy-start.2 = (bf16[1,128,1,4096]{3,1,2,0:T(8,128)(2,1)S(1)}, bf16[1,128,1,4096]{3,1,2,0:T(8,128)(2,1)}, u32[]{:S(2)}) copy-start(bf16[1,128,1,4096]{3,1,2,0:T(8,128)(2,1)} %param.12) | copy-start | bytes 3145732
  13.0 45.7 %all-to-all-start = ((bf16[16,48,1024]{2,1,0:T(8,128)(2,1)}), bf16[16,48,1024]{2,1,0:T(8,128)(2,1)S(1)}, u32[]{:S(2)}, u32[]{:S(2)}) async-start(bf16[16,48,1024]{2,1,0:T(8,128)(2,1)} %bitcast.5), calls=%async_computation | async-start | bytes 3145728 | tf_op jit(solution)/shard_map/all_to_all | solution.py:199
  22.8 47.2 %copy-start.6 = (bf16[1,128,1,512]{3,1,2,0:T(8,128)(2,1)S(1)}, bf16[1,128,1,512]{3,1,2,0:T(8,128)(2,1)}, u32[]{:S(2)}) copy-start(bf16[1,128,1,512]{3,1,2,0:T(8,128)(2,1)} %param.11) | copy-start | bytes 393220
  58.8 51.6 %all-to-all-start.1 = ((bf16[16,48,1024]{2,1,0:T(8,128)(2,1)}), bf16[16,48,1024]{2,1,0:T(8,128)(2,1)S(1)}, u32[]{:S(2)}, u32[]{:S(2)}) async-start(bf16[16,48,1024]{2,1,0:T(8,128)(2,1)} %bitcast.58), calls=%async_computation.1 | async-start | bytes 3145728 | tf_op jit(solution)/shard_map/all_to_all | solution.py:199
  136.9 41.5 %all-to-all-start.3 = ((bf16[16,128,256]{1,2,0:T(8,128)(2,1)}), bf16[16,128,256]{1,2,0:T(8,128)(2,1)}, u32[]{:S(2)}, u32[]{:S(2)}) async-start(bf16[16,128,256]{1,2,0:T(8,128)(2,1)} %bitcast.55), calls=%async_computation.3 | async-start | bytes 2097152 | tf_op jit(solution)/shard_map/all_to_all | solution.py:225
  141.3 0.6 copy-start.7
  150.7 45.7 %copy-start.9 = (s32[512]{0:T(512)S(1)}, s32[512]{0:T(512)}, u32[]{:S(2)}) copy-start(s32[512]{0:T(512)} %copy-done.8) | copy-start | bytes 6148
  177.7 0.8 copy-start
  197.1 9.3 %collective-permute-start = (bf16[1,128,512]{1,2,0:T(8,128)(2,1)S(1)}, bf16[1,128,512]{1,2,0:T(8,128)(2,1)S(1)}, u32[]{:S(2)}, u32[]{:S(2)}) collective-permute-start(bf16[1,128,512]{1,2,0:T(8,128)(2,1)S(1)} %fusion.68), channel_id=1, source_target_pairs={{0,16},{2,18},{4,20},{6,22},{8,24},{10,26},{12,28},{14,30},{16,0},... | collective-permute-start | bytes 393224 | tf_op jit(solution)/shard_map/ppermute | solution.py:151
  206.4 7.7 %collective-permute-start.1 = (bf16[2,128,512]{1,2,0:T(8,128)(2,1)S(1)}, bf16[2,128,512]{1,2,0:T(8,128)(2,1)S(1)}, u32[]{:S(2)}, u32[]{:S(2)}) collective-permute-start(bf16[2,128,512]{1,2,0:T(8,128)(2,1)S(1)} %pad_maximum_fusion.2), channel_id=1, source_target_pairs={{0,8},{2,10},{4,12},{6,14},{8,0},{10,2},{12,4},{14,6},{16,24},{18,... | collective-permute-start | bytes 786440 | tf_op jit(solution)/shard_map/ppermute | solution.py:151
  214.2 12.6 %collective-permute-start.2 = (bf16[4,128,512]{1,2,0:T(8,128)(2,1)S(1)}, bf16[4,128,512]{1,2,0:T(8,128)(2,1)}, u32[]{:S(2)}, u32[]{:S(2)}) collective-permute-start(bf16[4,128,512]{1,2,0:T(8,128)(2,1)S(1)} %pad_maximum_fusion.1), channel_id=1, source_target_pairs={{0,4},{2,6},{4,0},{6,2},{8,12},{10,14},{12,8},{14,10},{16,20},{18,... | collective-permute-start | bytes 1572872 | tf_op jit(solution)/shard_map/ppermute | solution.py:151
  227.9 8.9 %collective-permute-start.3 = (bf16[8,128,512]{1,2,0:T(8,128)(2,1)S(1)}, bf16[8,128,512]{1,2,0:T(8,128)(2,1)S(1)}, u32[]{:S(2)}, u32[]{:S(2)}) collective-permute-start(bf16[8,128,512]{1,2,0:T(8,128)(2,1)S(1)} %pad_maximum_fusion), channel_id=1, source_target_pairs={{0,2},{2,0},{4,6},{6,4},{8,10},{10,8},{12,14},{14,12},{16,18},{18,... | collective-permute-start | bytes 3145736 | tf_op jit(solution)/shard_map/ppermute | solution.py:151
  236.9 3.7 %copy-start.1 = (bf16[4096,512]{1,0:T(8,128)(2,1)S(1)}, bf16[4096,512]{1,0:T(8,128)(2,1)}, u32[]{:S(2)}) copy-start(bf16[4096,512]{1,0:T(8,128)(2,1)} %all-gather.2.cloned.1.call-done) | copy-start | bytes 12582916
  238.7 8.8 %copy-start.3 = (bf16[128,512]{1,0:T(8,128)(2,1)S(1)}, bf16[128,512]{1,0:T(8,128)(2,1)}, u32[]{:S(2)}) copy-start(bf16[128,512]{1,0:T(8,128)(2,1)} %param.13) | copy-start | bytes 393220
  238.7 8.8 %copy-start.4 = (f32[128,512]{1,0:T(8,128)S(1)}, f32[128,512]{1,0:T(8,128)}, u32[]{:S(2)}) copy-start(f32[128,512]{1,0:T(8,128)} %param.15) | copy-start | bytes 786436
  238.7 8.8 %copy-start.5 = (f32[128,512]{1,0:T(8,128)S(1)}, f32[128,512]{1,0:T(8,128)}, u32[]{:S(2)}) copy-start(f32[128,512]{1,0:T(8,128)} %param.14) | copy-start | bytes 786436
  238.7 8.8 %collective-permute-start.4 = (f32[128,512]{1,0:T(8,128)S(1)}, f32[128,512]{1,0:T(8,128)S(1)}, u32[]{:S(2)}, u32[]{:S(2)}) collective-permute-start(f32[128,512]{1,0:T(8,128)S(1)} %constant_dynamic-slice_fusion), channel_id=1, source_target_pairs={{0,1},{1,0},{2,3},{3,2},{4,5},{5,4},{6,7},{7,6},{8,9},{9,8},{10,11... | collective-permute-start | bytes 786440 | tf_op jit(solution)/shard_map/ppermute | solution.py:167
Sparse Core Ops, SparseCore 0:
  10.9 89.8 all-gather.1
